TPU v7x, 1024 devices: a whole 8x8x8 slice. The times are simulated.
1024 devices in a mesh: expert: 64 (over x_lo, z, core), mp: 16 (over x_hi, y).
Axes of the slice: x: 8 (x_hi: 2, x_lo: 4; x = x_hi * 4 + x_lo), y: 8, z: 8, core: 2. Of those that a mesh axis runs over, the one named last changes fastest.
Arguments:
- tokens: bfloat16 [8192, 2048], P('expert', 'mp'), may hold values from -6 to 6
- cotangent: bfloat16 [8192, 2048], P('expert', 'mp'), may hold values from -6 to 6
- expert_ids: int32 [8192], P('expert'), may hold values from 0 to 63, as said below
- slots: int32 [8192], P('expert'), may hold values from -1 to 3, as said below
- gate: float32 [8192], P('expert'), may hold values from 0.1 to 1
- w_in: bfloat16 [64, 2048, 6144], P('expert', None, 'mp'), may hold values from -0.125 to 0.125
- w_out: bfloat16 [64, 6144, 2048], P('expert', 'mp'), may hold values from -0.078125 to 0.078125
Outputs:
- input_grad: bfloat16 [8192, 2048], P('expert', 'mp')
Inputs may be any that keep to these rules, and one draw needn't show every extreme that they name: `expert_ids`: some expert receives exactly 4 kept tokens from every group of 128 tokens. `slots`: A kept token's slot is the number of earlier tokens of its group routed to the same expert; a token with 4 or more such earlier tokens has slot -1.
All inputs are finite; a program needn't handle non-finite values.
Results may differ from a plain program's by a relative error of at most 0.0057.
Values may be sent and summed in bfloat16 or wider, within the bound.
A program may use at most 32 MiB of HBM per device.

v0:
```python
import jax
import jax.numpy as jnp
from jax import lax
from jax.sharding import PartitionSpec as P


def gelu_slope(pre_act):
    coeff = 0.7978845608
    tanh_part = jnp.tanh(coeff * (pre_act + 0.044715 * pre_act * pre_act * pre_act))
    return 0.5 * (1.0 + tanh_part) + 0.5 * pre_act * (1.0 - tanh_part * tanh_part) * coeff * (
        1.0 + 3.0 * 0.044715 * pre_act * pre_act
    )


def local(tokens, cotangent, expert_ids, slots, gate, w_in, w_out):
    experts = lax.axis_size("expert")
    tok_count = tokens.shape[0]
    capacity = 2 * tok_count // experts
    slot_total = experts * capacity
    target = jnp.where(slots >= 0, expert_ids * capacity + slots, slot_total)
    scaled = (gate[:, None] * cotangent.astype(jnp.float32)).astype(jnp.bfloat16)
    weights_in = w_in[0]
    weights_out = w_out[0]
    onehot_table = (target[:, None] == jnp.arange(slot_total, dtype=jnp.int32)[None, :]).astype(
        jnp.bfloat16
    )
    stacked = jnp.stack([tokens, scaled])
    outgoing = (
        jnp.einsum("ts,ktd->ksd", onehot_table, stacked, preferred_element_type=jnp.float32)
        .astype(jnp.bfloat16)
        .reshape(2, experts, capacity, stacked.shape[2])
    )
    arrived = lax.all_to_all(outgoing, "expert", split_axis=1, concat_axis=1, tiled=True)
    shard_piece = lax.all_gather(arrived, "mp", axis=3, tiled=True)
    width = shard_piece.shape[3]
    inputs = shard_piece[0].reshape(slot_total, width)
    grads = shard_piece[1].reshape(slot_total, width)
    first = jnp.dot(inputs, weights_in, preferred_element_type=jnp.float32)
    second = lax.dot_general(
        grads, weights_out, (((1,), (1,)), ((), ())), preferred_element_type=jnp.float32
    )
    hidden_grad = (second * gelu_slope(first)).astype(jnp.bfloat16)
    summed = lax.psum_scatter(
        lax.dot_general(
            weights_in, hidden_grad, (((1,), (1,)), ((), ())), preferred_element_type=jnp.float32
        ),
        "mp",
        scatter_dimension=0,
        tiled=True,
    )
    expert_grad = summed.T.astype(jnp.bfloat16).reshape(experts, capacity, summed.shape[0])
    returned = lax.all_to_all(expert_grad, "expert", split_axis=0, concat_axis=0, tiled=True)
    return lax.dot_general(
        onehot_table,
        returned.reshape(slot_total, summed.shape[0]),
        (((1,), (0,)), ((), ())),
        preferred_element_type=jnp.float32,
    ).astype(jnp.bfloat16)


def solution(mesh):
    in_specs = (
        P("expert", "mp"),
        P("expert", "mp"),
        P("expert"),
        P("expert"),
        P("expert"),
        P("expert", None, "mp"),
        P("expert", "mp", None),
    )
    out_specs = P("expert", "mp")
    return jax.shard_map(local, mesh=mesh, in_specs=in_specs, out_specs=out_specs, check_vma=False)
```

profile of v0, /device:TPU:1, one launch (start us, length us, event | category | flops | bytes accessed | tf_op | source)
XLA Modules:
  0.0 395.3 jit_solution(1659275193019448457)
XLA Ops:
  6.5 0.0 copy-start
  6.5 0.0 all-gather.2.cloned.1.call-start
  6.5 1.0 copy.13
  7.5 0.9 copy.14
  8.4 0.7 compare_select_fusion
  9.1 0.7 fusion.40
  9.8 0.2 fusion.13
  10.0 0.1 copy.15
  10.2 31.4 %all_to_all.10 = bf16[2,64,4,128]{3,2,0,1:T(4,128)(2,1)} all-to-all(bf16[2,64,4,128]{3,2,0,1:T(4,128)(2,1)S(1)} %copy.16), channel_id=1, replica_groups=mesh['expert'=64,'mp'=16] {'expert'}, dimensions={1} | all-to-all | bytes 262144 | tf_op jit(solution)/shard_map/all_to_all | solution.py:33
  41.6 0.0 all-gather.2.cloned.1.call-update
  41.6 0.0 reduce-scatter.2.cloned.1.call-start
  41.7 77.1 %all-gather.2.cloned.1.call-done = bf16[2,64,4,2048]{3,2,0,1:T(4,128)(2,1)} async-done(((bf16[2,64,4,128]{3,2,0,1:T(4,128)(2,1)}), bf16[2,64,4,2048]{3,2,0,1:T(4,128)(2,1)}) %all-gather.2.cloned.1.call-update) | async-done | bytes 2097168 | tf_op jit(solution)/shard_map/all_gather | solution.py:34
  118.8 3.9 fusion.47
  122.7 1.3 reshape_squeeze.7
  124.0 2.1 reshape_squeeze.6
  126.1 0.0 copy-done
  126.1 0.7 fusion.1
  126.9 4.5 %convolution_bitcast_fusion = f32[2048,256]{0,1:T(8,128)} fusion(bf16[1,2048,384]{2,1,0:T(8,128)(2,1)S(1)} %copy-done, bf16[256,2048]{1,0:T(8,128)(2,1)} %reshape_squeeze.6, bf16[1,384,2048]{2,1,0:T(8,128)(2,1)} %param.13, f32[256,384]{1,0:T(8,128)S(1)} %fusion.1), kind=kOutput, calls=%fused_computation | convolution fusion | flops 807174144 | bytes 6684672 | tf_op jit(solution)/shard_map/dot_general | solution.py:44
  131.4 0.0 reduce-scatter.2.cloned.1.call-update
  131.4 230.8 %reduce-scatter.2.cloned.1.call-done = f32[128,256]{0,1:T(8,128)} async-done(((f32[2048,256]{0,1:T(8,128)}), f32[128,256]{0,1:T(8,128)}) %reduce-scatter.2.cloned.1.call-update) | async-done | bytes 131088 | tf_op jit(solution)/shard_map/reduce_scatter | solution.py:43
  362.2 0.9 convert_element_type.30
  363.2 24.4 %all_to_all.11 = bf16[64,4,128]{2,1,0:T(4,128)(2,1)S(1)} all-to-all(bf16[64,4,128]{2,1,0:T(4,128)(2,1)S(1)} %bitcast.37), channel_id=1, replica_groups=mesh['expert'=64,'mp'=16] {'expert'}, dimensions={0} | all-to-all | bytes 131072 | tf_op jit(solution)/shard_map/all_to_all | solution.py:52
  387.6 0.8 convolution_convert_fusion.1
  (1 shorter events, 0.0 us)
Async XLA Ops:
  6.5 119.6 %copy-start = (bf16[1,2048,384]{2,1,0:T(8,128)(2,1)S(1)}, bf16[1,2048,384]{2,1,0:T(8,128)(2,1)}, u32[]{:S(2)}) copy-start(bf16[1,2048,384]{2,1,0:T(8,128)(2,1)} %param.12) | copy-start | bytes 4718596
  6.5 112.3 %all-gather.2.cloned.1.call-start = ((), (), s32[]{:S(2)}) async-start(), calls=%async_computation.3 | async-start | bytes 2228224 | tf_op jit(solution)/shard_map/all_gather | solution.py:34
  41.6 320.6 %reduce-scatter.2.cloned.1.call-start = ((), (), s32[]{:S(2)}) async-start(), calls=%async_computation.4 | async-start | bytes 2228224 | tf_op jit(solution)/shard_map/reduce_scatter | solution.py:43
Sparse Core Ops, SparseCore 0:
  41.8 76.9 all-gather.1
  131.5 230.6 reduce-scatter.1
where the time goes:
time: 396 us; the launch traced here: 395 us
  waiting for transfers between devices  308 us (78%)
  blocking collectives  55.9 us (14%)
  between operations  13.4 us (3%)
  local copies, waits for them, and re-layouts  9.37 us (2%)
  matrix products  6.29 us (2%)
    reduce_scatter x1, waiting for transfers between devices, local(): lax.psum_scatter(lax.dot_general(weights_in, hidden_grad, (((1,), (1,)),...  231 us
    all_gather x1, waiting for transfers between devices, local(): shard_piece = lax.all_gather(arrived, 'mp', axis=3, tiled=True)  77.1 us
    all_to_all x1, blocking collectives, local(): lax.all_to_all(outgoing, 'expert', split_axis=1, concat_axis=1, tiled=True)  31.4 us
    all_to_all x1, blocking collectives, local(): lax.all_to_all(expert_grad, 'expert', split_axis=0, concat_axis=0, tiled=...  24.4 us
  transfers between devices with their start and end apart: 2, of which 2 were waited for; matrix products, arithmetic and copies ran while one was open for 0% of the time, Pallas kernels for 0%

commit v1 on v0

v1 whole, which is shorter than its diff:
```python
import functools

import jax
import jax.numpy as jnp
from jax import lax
from jax.experimental import pallas as pl
from jax.experimental.pallas import tpu as pltpu
from jax.sharding import PartitionSpec as P

MESH = pl.DeviceIdType.MESH
F32 = jnp.float32
BF16 = jnp.bfloat16
CAP = 4
XH = 2
XL = 4


def gelu_slope(pre_act):
    coeff = 0.7978845608
    square = pre_act * pre_act
    tanh_part = jnp.tanh(coeff * (pre_act + 0.044715 * square * pre_act))
    return 0.5 * (1.0 + tanh_part) + 0.5 * pre_act * (1.0 - tanh_part * tanh_part) * coeff * (
        1.0 + 3.0 * 0.044715 * square
    )


def dot(a, b, dims=((1,), (0,))):
    return lax.dot_general(a, b, (dims, ((), ())), preferred_element_type=F32)


def kernel(
    XL, Y, ZC,
    tok_ref, cot_ref, ids_ref, slots_ref, gate_ref, win_hbm, wout_hbm,
    out_ref,
    win, wout, s1, r1, s2, g, pre, inner, hg, pf, u, q, fin, back, eg, s4, r4,
    wsem, z1s, z1r, x1s, x1r, ys, yr, rs, rr, x2s, x2r, z2s, z2r,
):
    X = XH * XL
    H = Y // 2
    tokens, feat = tok_ref.shape
    rows = ZC * CAP
    total = XL * rows
    span = XL * CAP

    expert = lax.axis_index("expert")
    mp = lax.axis_index("mp")
    x_lo, zc = lax.div(expert, ZC), lax.rem(expert, ZC)
    x_hi, y = lax.div(mp, Y), lax.rem(mp, Y)
    x = x_hi * XL + x_lo

    def at_zc(j):
        return (x_lo * ZC + lax.rem(zc + j, ZC), mp)

    def at_x(j):
        px = lax.rem(x + j, X)
        return (lax.rem(px, XL) * ZC + zc, lax.div(px, XL) * Y + y)

    def at_y(j):
        return (expert, x_hi * Y + lax.rem(y + Y + j, Y))

    loads = []
    for h in range(XH):
        loads.append(pltpu.make_async_copy(win_hbm.at[h], win.at[:, h], wsem.at[len(loads)]))
        for k in range(Y):
            loads.append(
                pltpu.make_async_copy(
                    wout_hbm.at[:, pl.ds((h * Y + k) * feat, feat)], wout.at[k, h], wsem.at[len(loads)]
                )
            )
    for load in loads:
        load.start()

    barrier = pltpu.get_barrier_semaphore()
    peers = [at_zc(j) for j in range(1, ZC)] + [at_x(j) for j in range(1, X)] + [at_y(1), at_y(-1)]
    for peer in peers:
        pl.semaphore_signal(barrier, inc=1, device_id=peer, device_id_type=MESH)

    ids, slots = ids_ref[...], slots_ref[...]
    target = jnp.where(
        slots >= 0, lax.rem(ids, ZC) * span + lax.div(ids, ZC) * CAP + slots, total
    )
    onehot = jnp.where(
        lax.broadcasted_iota(jnp.int32, (total, tokens), 0) == target, 1.0, 0.0
    ).astype(BF16)
    eye = lax.broadcasted_iota(jnp.int32, (tokens, tokens), 0) == lax.broadcasted_iota(
        jnp.int32, (tokens, tokens), 1
    )
    gate = jnp.sum(jnp.where(eye, gate_ref[...], 0.0), axis=1, keepdims=True)
    scaled = (gate * cot_ref[...].astype(F32)).astype(BF16)
    s1[0] = dot(onehot, tok_ref[...]).astype(BF16)
    s1[1] = dot(onehot, scaled).astype(BF16)

    pl.semaphore_wait(barrier, len(peers))

    def zc_rows(j):
        return pl.ds(pl.multiple_of(lax.rem(zc + j, ZC) * span, span), span)

    sends = []

    def send(src, dst, ssem, rsem, dev):
        copy = pltpu.make_async_remote_copy(
            src_ref=src, dst_ref=dst, send_sem=ssem, recv_sem=rsem, device_id=dev, device_id_type=MESH
        )
        copy.start()
        sends.append(copy)

    def arrive(dst, ssem, rsem, dev):
        pltpu.make_async_remote_copy(
            src_ref=dst, dst_ref=dst, send_sem=ssem, recv_sem=rsem, device_id=dev, device_id_type=MESH
        ).wait_recv()

    for j in range(1, ZC):
        send(s1.at[:, zc_rows(j)], r1.at[:, zc_rows(0)], z1s.at[j], z1r.at[j], at_zc(j))
    r1[:, zc_rows(0)] = s1[:, zc_rows(0)]

    ro = lax.broadcasted_iota(jnp.int32, (total, total), 0)
    ri = lax.broadcasted_iota(jnp.int32, (total, total), 1)
    ro_in = (
        lax.rem(lax.div(ro, CAP), ZC) * span + lax.div(ro, rows) * CAP + lax.rem(ro, CAP)
    )
    perm = jnp.where(ro_in == ri, 1.0, 0.0).astype(BF16)

    for j in range(1, ZC):
        arrive(r1.at[:, zc_rows(ZC - j)], z1s.at[j], z1r.at[j], at_zc(j))
    for t in range(2):
        s2[t] = dot(perm, r1[t]).astype(BF16).reshape(XL, rows, feat)

    order = [XL] + [j for d in range(1, XL) for j in (X - d, XL - d)]
    for j in order:
        px = lax.rem(x + j, X)
        send(
            s2.at[:, lax.rem(px, XL)], g.at[:, y, x_lo, x_hi], x1s.at[j], x1r.at[j], at_x(j)
        )
    g[:, y, x_lo, x_hi] = s2[:, x_lo]

    hops = ((H, H - 1), (H - 1, H))
    step = (1, -1)

    def ring_send(way, t, hop, c):
        yb = lax.rem(y + Y - step[way] * (hop - 1), Y)
        ref = g.at[t, yb, c]
        send(ref, ref, ys.at[way, t, hop - 1, c], yr.at[way, t, hop - 1, c], at_y(step[way]))

    def ring_arrive(way, t, hop, c):
        yb = lax.rem(y + Y - step[way] * hop, Y)
        arrive(
            g.at[t, yb, c], ys.at[way, t, hop - 1, c], yr.at[way, t, hop - 1, c], at_y(step[way])
        )

    def block(t, yb):
        return jnp.concatenate(
            [jnp.concatenate([g[t, yb, c, h] for h in range(XH)], axis=1) for c in range(XL)], axis=0
        )

    def weights(ref, yb, axis):
        return jnp.concatenate([ref[yb, h] for h in range(XH)], axis=axis)

    def accumulate(yb, first=False):
        a = dot(block(0, yb), weights(win, yb, 0))
        b = dot(block(1, yb), weights(wout, yb, 1), ((1,), (1,)))
        if first:
            pre[...], inner[...] = a, b
        else:
            pre[...] += a
            inner[...] += b

    chunks = [lax.rem(x_lo + d, XL) for d in range(XL)]
    for d in range(XL):
        for j in ([XL] if d == 0 else [X - d, XL - d]):
            src = lax.rem(x + X - j, X)
            arrive(
                g.at[:, y, lax.rem(src, XL), lax.div(src, XL)], x1s.at[j], x1r.at[j], at_x(j)
            )
        for t in range(2):
            for way in range(2):
                ring_send(way, t, 1, chunks[d])
    for load in loads:
        load.wait()
    accumulate(y, True)
    for hop in range(1, H + 1):
        for c in chunks:
            for t in range(2):
                for way in range(2):
                    if hop <= hops[way][t]:
                        ring_arrive(way, t, hop, c)
                        if hop < hops[way][t]:
                            ring_send(way, t, hop + 1, c)
        accumulate(lax.rem(y + hop, Y))
        if hop < H:
            accumulate(lax.rem(y + Y - hop, Y))

    hg[...] = (inner[...] * gelu_slope(pre[...])).astype(BF16)

    halves = (range(XL // 2), range(XL // 2, XL))
    start = ((H, H - 1), (H - 1, H))

    def partial(slot, yb):
        value = dot(hg[...], weights(win, yb, 0), ((1,), (1,)))
        for c in range(XL):
            for h in range(XH):
                pf[slot, c, h] = value[c * rows:(c + 1) * rows, h * feat:(h + 1) * feat]

    def sum_send(way, half, k, slot):
        for c in halves[half]:
            if k < start[way][half]:
                arrive(q.at[way, k, c], rs.at[way, k, c], rr.at[way, k, c], at_y(step[way]))
                u[way, k - 1, c] = (pf[slot, c] + q[way, k, c].astype(F32)).astype(BF16)
            else:
                u[way, k - 1, c] = pf[slot, c].astype(BF16)
            send(
                u.at[way, k - 1, c], q.at[way, k - 1, c], rs.at[way, k - 1, c], rr.at[way, k - 1, c],
                at_y(step[way]),
            )

    partial(0, lax.rem(y + H, Y))
    sum_send(0, 0, H, 0)
    sum_send(1, 1, H, 0)
    for k in range(H - 1, 0, -1):
        partial(2 * k - 1, lax.rem(y + k, Y))
        partial(2 * k, lax.rem(y + Y - k, Y))
        sum_send(0, 1, k, 2 * k - 1)
        sum_send(1, 0, k, 2 * k)
        sum_send(0, 0, k, 2 * k - 1)
        sum_send(1, 1, k, 2 * k)
    partial(0, y)
    for c in range(XL):
        value = pf[0, c]
        for way in range(2):
            arrive(q.at[way, 0, c], rs.at[way, 0, c], rr.at[way, 0, c], at_y(step[way]))
            value += q[way, 0, c].astype(F32)
        fin[c] = value.astype(BF16)

    for j in order:
        px = lax.rem(x + j, X)
        send(fin.at[lax.rem(px, XL), lax.div(px, XL)], back.at[j], x2s.at[j], x2r.at[j], at_x(j))
    back[0] = fin[x_lo, x_hi]
    for j in range(XL):
        for k in (j, j + XL):
            if k:
                arrive(back.at[k], x2s.at[k], x2r.at[k], at_x(k))
        eg[lax.rem(x_lo + XL - j, XL)] = (
            back[j].astype(F32) + back[j + XL].astype(F32)
        ).astype(BF16)
    s4[...] = dot(perm, eg[...].reshape(total, feat), ((0,), (0,))).astype(BF16)

    for j in range(1, ZC):
        send(s4.at[zc_rows(j)], r4.at[zc_rows(0)], z2s.at[j], z2r.at[j], at_zc(j))
    r4[zc_rows(0)] = s4[zc_rows(0)]
    for j in range(1, ZC):
        arrive(r4.at[zc_rows(ZC - j)], z2s.at[j], z2r.at[j], at_zc(j))
    out_ref[...] = dot(onehot, r4[...], ((0,), (0,))).astype(BF16)
    for copy in sends:
        copy.wait_send()


def local(XL, Y, ZC, tokens, cotangent, expert_ids, slots, gate, w_in, w_out):
    count, feat = tokens.shape
    hidden = w_in.shape[2]
    H = Y // 2
    rows = ZC * CAP
    total = XL * rows
    vmem = pl.BlockSpec(memory_space=pltpu.VMEM)
    hbm = pl.BlockSpec(memory_space=pl.ANY)
    dma = pltpu.SemaphoreType.DMA
    return pl.pallas_call(
        functools.partial(kernel, XL, Y, ZC),
        out_shape=jax.ShapeDtypeStruct((count, feat), BF16),
        in_specs=[vmem] * 5 + [hbm] * 2,
        out_specs=vmem,
        scratch_shapes=[
            pltpu.VMEM((Y, XH, feat, hidden), BF16),
            pltpu.VMEM((Y, XH, hidden, feat), BF16),
            pltpu.VMEM((2, total, feat), BF16),
            pltpu.VMEM((2, total, feat), BF16),
            pltpu.VMEM((2, XL, rows, feat), BF16),
            pltpu.VMEM((2, Y, XL, XH, rows, feat), BF16),
            pltpu.VMEM((total, hidden), F32),
            pltpu.VMEM((total, hidden), F32),
            pltpu.VMEM((total, hidden), BF16),
            pltpu.VMEM((2 * H - 1, XL, XH, rows, feat), F32),
            pltpu.VMEM((2, H, XL, XH, rows, feat), BF16),
            pltpu.VMEM((2, H, XL, XH, rows, feat), BF16),
            pltpu.VMEM((XL, XH, rows, feat), BF16),
            pltpu.VMEM((XH * XL, rows, feat), BF16),
            pltpu.VMEM((XL, rows, feat), BF16),
            pltpu.VMEM((total, feat), BF16),
            pltpu.VMEM((total, feat), BF16),
            dma((XH * (Y + 1),)),
            dma((ZC,)), dma((ZC,)),
            dma((XH * XL,)), dma((XH * XL,)),
            dma((2, 2, H, XL)), dma((2, 2, H, XL)),
            dma((2, H, XL)), dma((2, H, XL)),
            dma((XH * XL,)), dma((XH * XL,)),
            dma((ZC,)), dma((ZC,)),
        ],
        compiler_params=pltpu.CompilerParams(
            collective_id=0, has_side_effects=True, vmem_limit_bytes=40 * 1024 * 1024
        ),
        cost_estimate=pl.CostEstimate(
            flops=6 * total * w_in.shape[1] * hidden,
            bytes_accessed=4 * w_in.shape[1] * hidden,
            transcendentals=total * hidden,
        ),
    )(
        tokens,
        cotangent,
        expert_ids.reshape(1, count),
        slots.reshape(1, count),
        gate.reshape(1, count),
        w_in.reshape(XH, Y, feat, hidden),
        w_out.reshape(hidden, XH * Y * feat),
    )


def solution(mesh):
    in_specs = (
        P("expert", "mp"),
        P("expert", "mp"),
        P("expert"),
        P("expert"),
        P("expert"),
        P("expert", None, "mp"),
        P("expert", "mp", None),
    )
    return jax.shard_map(
        functools.partial(local, XL, mesh.shape["mp"] // XH, mesh.shape["expert"] // XL),
        mesh=mesh,
        in_specs=in_specs,
        out_specs=P("expert", "mp"),
        check_vma=False,
    )
```

time: 396 us -> 93.3 us (0.24)
  waiting for transfers between devices: 308 us -> 0 us
  Pallas kernels: 0 us -> 86 us
  blocking collectives: 55.9 us -> 0 us
  between operations: 13.4 us -> 0.02 us
  matrix products: 6.29 us -> 0 us
    reduce_scatter x1 -> x0, waiting for transfers between devices: 231 us -> none  [local(): lax.psum_scatter(lax.dot_general(weights_in, hidden_grad, (((1,), (1,)),...]
    pallas_call x0 -> x1, Pallas kernels: none -> 86 us  [local(): pl.pallas_call(functools.partial(kernel, XL, Y, ZC), out_shape=jax.ShapeD...]
    all_gather x1 -> x0, waiting for transfers between devices: 77.1 us -> none  [local(): shard_piece = lax.all_gather(arrived, 'mp', axis=3, tiled=True)]
    all_to_all x2 -> x0, blocking collectives: 55.9 us -> none  [the longest x1 31.4 us: local(): lax.all_to_all(outgoing, 'expert', split_axis=1, concat_axis=1, tiled=True)]
    dot_general x4 -> x0, matrix products: 6.29 us -> none  [the longest x1 4.51 us: local(): lax.dot_general(weights_in, hidden_grad, (((1,), (1,)), ((), ())), prefer...]
    unnamed x4 -> x15, local copies, waits for them, and re-layouts: 1.85 us -> 6.91 us
  transfers between devices with their start and end apart: 2 -> 0, of which waited for: 2 -> 0; matrix products, arithmetic and copies ran while one was open for 0% -> 0% of each run, Pallas kernels for 0% -> 0%
where the time goes in v1:
time: 93.3 us; the launch traced here: 92.9 us
  Pallas kernels  86 us (92%)
  local copies, waits for them, and re-layouts  6.91 us (7%)
    pallas_call x1, Pallas kernels, local(): pl.pallas_call(functools.partial(kernel, XL, Y, ZC), out_shape=jax.ShapeD...  86 us
    unnamed x15, local copies, waits for them, and re-layouts  6.91 us

profile of v1, /device:TPU:1, one launch (start us, length us, event | category | flops | bytes accessed | tf_op | source)
XLA Modules:
  0.0 92.9 jit_solution(4657746953186919813)
XLA Ops:
  0.0 0.0 copy-start
  0.0 1.4 %copy-done = bf16[1,2048,384]{2,1,0:T(8,128)(2,1)S(1)} copy-done((bf16[1,2048,384]{2,1,0:T(8,128)(2,1)S(1)}, bf16[1,2048,384]{2,1,0:T(8,128)(2,1)}, u32[]{:S(2)}) %copy-start) | copy-done | bytes 1572888
  1.4 0.0 copy-start.1
  1.4 1.4 %copy-done.1 = bf16[1,384,2048]{2,1,0:T(8,128)(2,1)S(1)} copy-done((bf16[1,384,2048]{2,1,0:T(8,128)(2,1)S(1)}, bf16[1,384,2048]{2,1,0:T(8,128)(2,1)}, u32[]{:S(2)}) %copy-start.1) | copy-done | bytes 1572888
  2.8 0.0 copy-start.2
  2.8 0.8 copy-done.2
  3.6 0.0 copy-start.3
  3.6 0.8 copy-done.3
  4.3 0.0 copy-start.4
  4.3 0.7 copy-done.4
  5.0 0.0 copy-start.5
  5.0 0.7 copy-done.5
  5.6 0.0 copy-start.6
  5.6 0.7 copy-done.6
  6.3 86.0 %shard_map.73 = bf16[128,128]{1,0:T(8,128)(2,1)S(1)} custom-call(bf16[128,128]{1,0:T(8,128)(2,1)S(1)} %copy-done.2, bf16[128,128]{1,0:T(8,128)(2,1)S(1)} %copy-done.3, s32[1,128]{1,0:T(1,128)S(1)} %bitcast.7, s32[1,128]{1,0:T(1,128)S(1)} %bitcast.8, f32[1,128]{1,0:T(1,128)S(1)} %bitcast.9, bf16[2,8,128,384]{3,2,1,0:T(8,128)(2,1)S(1)} %bitcast.5, ...), custom_call_target="tpu_custom_call" | custom-call | flops 1207959552 | bytes 3145728 | tf_op jit(solution)/shard_map/pallas_call | solution.py:265
  92.3 0.6 copy.9
Async XLA Ops:
  0.0 1.4 %copy-start = (bf16[1,2048,384]{2,1,0:T(8,128)(2,1)S(1)}, bf16[1,2048,384]{2,1,0:T(8,128)(2,1)}, u32[]{:S(2)}) copy-start(bf16[1,2048,384]{2,1,0:T(8,128)(2,1)} %param.12) | copy-start | bytes 4718596
  1.4 1.4 %copy-start.1 = (bf16[1,384,2048]{2,1,0:T(8,128)(2,1)S(1)}, bf16[1,384,2048]{2,1,0:T(8,128)(2,1)}, u32[]{:S(2)}) copy-start(bf16[1,384,2048]{2,1,0:T(8,128)(2,1)} %param.13) | copy-start | bytes 4718596
  2.8 0.8 copy-start.2
  3.6 0.8 copy-start.3
  4.3 0.7 copy-start.4
  5.0 0.7 copy-start.5
  5.6 0.7 copy-start.6

commit v2 on v1

v2 whole, which is shorter than its diff:
```python
import functools

import jax
import jax.numpy as jnp
from jax import lax
from jax.experimental import pallas as pl
from jax.experimental.pallas import tpu as pltpu
from jax.sharding import PartitionSpec as P

MESH = pl.DeviceIdType.MESH
F32 = jnp.float32
BF16 = jnp.bfloat16
CAP = 4
WAVE = 4
GROUP = 2
VMEM_LIMIT = 63 * 1024 * 1024
XH = 2
XL = 4


def gelu_slope(pre_act):
    coeff = 0.7978845608
    square = pre_act * pre_act
    tanh_part = jnp.tanh(coeff * (pre_act + 0.044715 * square * pre_act))
    return 0.5 * (1.0 + tanh_part) + 0.5 * pre_act * (1.0 - tanh_part * tanh_part) * coeff * (
        1.0 + 3.0 * 0.044715 * square
    )


def dot(a, b, dims=((1,), (0,))):
    return lax.dot_general(a, b, (dims, ((), ())), preferred_element_type=F32)


def kernel(
    XL, Y, ZC,
    tok_hbm, cot_hbm, ids_hbm, slots_hbm, gate_hbm, win_hbm, wout_hbm,
    out_ref,
    tok_ref, cot_ref, ids_ref, slots_ref, gate_ref,
    win, wout, s1, r1, s2, g, pre, inner, hg, pf, u, q, fin, back, eg, s4, r4,
    isem, wsem, ssem, z1r, x1r, yr, rr, x2r, z2r,
):
    X = XH * XL
    H = Y // 2
    tokens, feat = tok_hbm.shape
    rows = ZC * CAP
    total = XL * rows
    span = XL * CAP

    expert = lax.axis_index("expert")
    mp = lax.axis_index("mp")
    x_lo, zc = lax.div(expert, ZC), lax.rem(expert, ZC)
    x_hi, y = lax.div(mp, Y), lax.rem(mp, Y)
    x = x_hi * XL + x_lo

    def at_zc(j):
        return (x_lo * ZC + lax.rem(zc + j, ZC), mp)

    def at_x(j):
        px = lax.rem(x + j, X)
        return (lax.rem(px, XL) * ZC + zc, lax.div(px, XL) * Y + y)

    def at_y(j):
        return (expert, x_hi * Y + lax.rem(y + Y + j, Y))

    def unit(j):
        px = lax.rem(x + X + j, X)
        return lax.rem(px, XL) * XH + lax.div(px, XL)

    def send(src, dst, sems, rsem, dev):
        pltpu.make_async_remote_copy(
            src_ref=src, dst_ref=dst, send_sem=sems, recv_sem=rsem, device_id=dev, device_id_type=MESH
        ).start()

    def arrive(dst, sems, rsem, dev):
        pltpu.make_async_remote_copy(
            src_ref=dst, dst_ref=dst, send_sem=sems, recv_sem=rsem, device_id=dev, device_id_type=MESH
        ).wait_recv()

    def sent(src, sems, dev):
        pltpu.make_async_remote_copy(
            src_ref=src, dst_ref=src, send_sem=sems, recv_sem=sems, device_id=dev, device_id_type=MESH
        ).wait_send()

    small = []
    for src, dst in (
        (ids_hbm, ids_ref), (slots_hbm, slots_ref), (gate_hbm, gate_ref), (tok_hbm, tok_ref), (cot_hbm, cot_ref)
    ):
        small.append(pltpu.make_async_copy(src, dst, isem.at[len(small)]))
        small[-1].start()

    barrier = pltpu.get_barrier_semaphore()
    peers = [at_zc(j) for j in range(1, ZC)] + [at_x(j) for j in range(1, X)] + [at_y(1), at_y(-1)]
    for peer in peers:
        pl.semaphore_signal(barrier, inc=1, device_id=peer, device_id_type=MESH)

    loads = []
    for h in range(XH):
        loads.append(pltpu.make_async_copy(win_hbm.at[h], win.at[:, h], wsem.at[len(loads)]))
        for k in range(Y):
            loads.append(
                pltpu.make_async_copy(
                    wout_hbm.at[:, pl.ds((h * Y + k) * feat, feat)], wout.at[k, h], wsem.at[len(loads)]
                )
            )
    for load in small:
        load.wait()

    ids, slots = ids_ref[...], slots_ref[...]
    target = jnp.where(
        slots >= 0, lax.rem(ids, ZC) * span + lax.div(ids, ZC) * CAP + slots, total
    )
    onehot = jnp.where(
        lax.broadcasted_iota(jnp.int32, (total, tokens), 0) == target, 1.0, 0.0
    ).astype(BF16)
    eye = lax.broadcasted_iota(jnp.int32, (tokens, tokens), 0) == lax.broadcasted_iota(
        jnp.int32, (tokens, tokens), 1
    )
    gate = jnp.sum(jnp.where(eye, gate_ref[...], 0.0), axis=1, keepdims=True)
    scaled = (gate * cot_ref[...].astype(F32)).astype(BF16)
    s1[0] = dot(onehot, tok_ref[...]).astype(BF16)
    s1[1] = dot(onehot, scaled).astype(BF16)

    pl.semaphore_wait(barrier, len(peers))

    def zc_rows(j):
        return pl.ds(pl.multiple_of(lax.rem(zc + j, ZC) * span, span), span)

    others = pl.ds(0, total - span)
    for j in range(1, ZC):
        send(s1.at[:, zc_rows(j)], r1.at[:, zc_rows(0)], ssem.at[0], z1r.at[0], at_zc(j))
    r1[:, zc_rows(0)] = s1[:, zc_rows(0)]
    for load in loads:
        load.start()

    ro = lax.broadcasted_iota(jnp.int32, (total, total), 0)
    ri = lax.broadcasted_iota(jnp.int32, (total, total), 1)
    ro_in = (
        lax.rem(lax.div(ro, CAP), ZC) * span + lax.div(ro, rows) * CAP + lax.rem(ro, CAP)
    )
    perm = jnp.where(ro_in == ri, 1.0, 0.0).astype(BF16)

    arrive(r1.at[:, others], ssem.at[0], z1r.at[0], at_zc(1))
    for t in range(2):
        s2[t] = dot(perm, r1[t]).astype(BF16).reshape(XL, rows, feat)

    near = sorted(range(X), key=lambda j: min(j, X - j))
    for j in near[1:]:
        px = lax.rem(x + j, X)
        send(s2.at[:, lax.rem(px, XL)], g.at[:, y, unit(0)], ssem.at[1], x1r.at[j], at_x(j))
    g[:, y, unit(0)] = s2[:, x_lo]

    step = (1, -1)

    def ring(way, hop, j, forward):
        yb = lax.rem(y + Y - step[way] * (hop - forward), Y)
        ref = g.at[way, yb, unit(-j)] if hop == H else g.at[:, yb, unit(-j)]
        args = (ref, ssem.at[2], yr.at[way, hop - 1, j], at_y(step[way]))
        if forward:
            send(ref, *args)
        else:
            arrive(*args)

    def block(t, yb):
        return jnp.concatenate(
            [jnp.concatenate([g[t, yb, c * XH + h] for h in range(XH)], axis=1) for c in range(XL)], axis=0
        )

    def weights(ref, yb, axis):
        return jnp.concatenate([ref[yb, h] for h in range(XH)], axis=axis)

    def accumulate(yb, first=False):
        a = dot(block(0, yb), weights(win, yb, 0))
        b = dot(block(1, yb), weights(wout, yb, 1), ((1,), (1,)))
        if first:
            pre[...], inner[...] = a, b
        else:
            pre[...] += a
            inner[...] += b

    waves = [near[i:i + WAVE] for i in range(0, X, WAVE)]
    for j in near:
        if j:
            arrive(g.at[:, y, unit(-j)], ssem.at[1], x1r.at[j], at_x(j))
        for way in range(2):
            ring(way, 1, j, 1)
    for hop in range(1, H + 1):
        for wave in waves:
            for j in wave:
                for way in range(2):
                    ring(way, hop, j, 0)
                    if hop < H:
                        ring(way, hop + 1, j, 1)
            if hop == 1 and wave is waves[0]:
                for load in loads:
                    load.wait()
                accumulate(y, True)
        accumulate(lax.rem(y + hop, Y))
        if hop < H:
            accumulate(lax.rem(y + Y - hop, Y))

    hg[...] = (inner[...] * gelu_slope(pre[...])).astype(BF16)

    far = near[::-1]
    groups = range(0, X, GROUP)

    def partial(slot, yb):
        value = dot(hg[...], weights(win, yb, 0), ((1,), (1,)))
        for c in range(XL):
            for h in range(XH):
                pf[slot, c * XH + h] = value[c * rows:(c + 1) * rows, h * feat:(h + 1) * feat]

    def landed(way, k, p):
        arrive(
            q.at[way, k, pl.ds(p, GROUP)], ssem.at[3], rr.at[way, k, p // GROUP], at_y(step[way])
        )

    def sum_send(first, k, slot):
        for p in groups:
            way = (p // GROUP + (not first)) % 2
            fresh = k == (H if first else H - 1)
            if not fresh:
                landed(way, k, p)
            for i in range(p, p + GROUP):
                value = pf[slot + way * (k < H), unit(far[i])]
                if not fresh:
                    value += q[way, k, i].astype(F32)
                u[way, k - 1, i] = value.astype(BF16)
            send(
                u.at[way, k - 1, pl.ds(p, GROUP)], q.at[way, k - 1, pl.ds(p, GROUP)],
                ssem.at[3], rr.at[way, k - 1, p // GROUP], at_y(step[way]),
            )

    def partials(k):
        for way in range(2):
            partial(2 * k - 1 + way, lax.rem(y + Y + step[way] * k, Y))

    partial(2 * H - 1, lax.rem(y + H, Y))
    sum_send(True, H, 2 * H - 1)
    for k in range(H - 1, 0, -1):
        partials(k)
        sum_send(False, k, 2 * k - 1)
        sum_send(True, k, 2 * k - 1)
    partial(0, y)
    for p in groups:
        for way in range(2):
            landed(way, 0, p)
        for i in range(p, p + GROUP):
            j = far[i]
            value = (
                pf[0, unit(j)] + q[0, 0, i].astype(F32) + q[1, 0, i].astype(F32)
            ).astype(BF16)
            if j:
                fin[i] = value
                send(fin.at[i], back.at[j], ssem.at[4], x2r.at[j], at_x(j))
            else:
                back[0] = value

    for j in range(XL):
        for k in (j, j + XL):
            if k:
                arrive(back.at[k], ssem.at[4], x2r.at[k], at_x(k))
        eg[lax.rem(x_lo + XL - j, XL)] = (
            back[j].astype(F32) + back[j + XL].astype(F32)
        ).astype(BF16)
    s4[...] = dot(perm, eg[...].reshape(total, feat), ((0,), (0,))).astype(BF16)

    for j in range(1, ZC):
        send(s4.at[zc_rows(j)], r4.at[zc_rows(0)], ssem.at[5], z2r.at[0], at_zc(j))
    r4[zc_rows(0)] = s4[zc_rows(0)]
    sent(s1.at[:, others], ssem.at[0], at_zc(1))
    sent(g.at[:, 0, pl.ds(0, X - 1)], ssem.at[1], at_x(1))
    sent(g.at[:, pl.ds(0, Y - 1)], ssem.at[2], at_y(1))
    sent(u.at[:, :, pl.ds(0, X * (Y - 1) // Y)], ssem.at[3], at_y(1))
    sent(fin.at[pl.ds(0, X - 1)], ssem.at[4], at_x(1))
    arrive(r4.at[others], ssem.at[5], z2r.at[0], at_zc(1))
    out_ref[...] = dot(onehot, r4[...], ((0,), (0,))).astype(BF16)
    sent(s4.at[others], ssem.at[5], at_zc(1))


def local(XL, Y, ZC, tokens, cotangent, expert_ids, slots, gate, w_in, w_out):
    count, feat = tokens.shape
    hidden = w_in.shape[2]
    X, H = XH * XL, Y // 2
    rows = ZC * CAP
    total = XL * rows
    vmem = pl.BlockSpec(memory_space=pltpu.VMEM)
    hbm = pl.BlockSpec(memory_space=pl.ANY)
    dma = pltpu.SemaphoreType.DMA
    return pl.pallas_call(
        functools.partial(kernel, XL, Y, ZC),
        out_shape=jax.ShapeDtypeStruct((count, feat), BF16),
        in_specs=[hbm] * 7,
        out_specs=vmem,
        scratch_shapes=[
            pltpu.VMEM((count, feat), BF16),
            pltpu.VMEM((count, feat), BF16),
            pltpu.VMEM((1, count), jnp.int32),
            pltpu.VMEM((1, count), jnp.int32),
            pltpu.VMEM((1, count), F32),
            pltpu.VMEM((Y, XH, feat, hidden), BF16),
            pltpu.VMEM((Y, XH, hidden, feat), BF16),
            pltpu.VMEM((2, total, feat), BF16),
            pltpu.VMEM((2, total, feat), BF16),
            pltpu.VMEM((2, XL, rows, feat), BF16),
            pltpu.VMEM((2, Y, X, rows, feat), BF16),
            pltpu.VMEM((total, hidden), F32),
            pltpu.VMEM((total, hidden), F32),
            pltpu.VMEM((total, hidden), BF16),
            pltpu.VMEM((Y, X, rows, feat), F32),
            pltpu.VMEM((2, H, X, rows, feat), BF16),
            pltpu.VMEM((2, H, X, rows, feat), BF16),
            pltpu.VMEM((X, rows, feat), BF16),
            pltpu.VMEM((X, rows, feat), BF16),
            pltpu.VMEM((XL, rows, feat), BF16),
            pltpu.VMEM((total, feat), BF16),
            pltpu.VMEM((total, feat), BF16),
            dma((5,)),
            dma((XH * (Y + 1),)),
            dma((6,)),
            dma((1,)),
            dma((X,)),
            dma((2, H, X)),
            dma((2, H, X // GROUP)),
            dma((X,)),
            dma((1,)),
        ],
        compiler_params=pltpu.CompilerParams(
            collective_id=0, has_side_effects=True, vmem_limit_bytes=VMEM_LIMIT
        ),
        cost_estimate=pl.CostEstimate(
            flops=6 * total * w_in.shape[1] * hidden,
            bytes_accessed=4 * w_in.shape[1] * hidden,
            transcendentals=total * hidden,
        ),
    )(
        tokens,
        cotangent,
        expert_ids.reshape(1, count),
        slots.reshape(1, count),
        gate.reshape(1, count),
        w_in.reshape(XH, Y, feat, hidden),
        w_out.reshape(hidden, XH * Y * feat),
    )


def solution(mesh):
    in_specs = (
        P("expert", "mp"),
        P("expert", "mp"),
        P("expert"),
        P("expert"),
        P("expert"),
        P("expert", None, "mp"),
        P("expert", "mp", None),
    )
    return jax.shard_map(
        functools.partial(local, XL, mesh.shape["mp"] // XH, mesh.shape["expert"] // XL),
        mesh=mesh,
        in_specs=in_specs,
        out_specs=P("expert", "mp"),
        check_vma=False,
    )
```

time: 93.3 us -> 84.1 us (0.901)
  local copies, waits for them, and re-layouts: 6.91 us -> 1.38 us
  Pallas kernels: 86 us -> 82.5 us
    unnamed x15 -> x1, local copies, waits for them, and re-layouts: 6.91 us -> 1.38 us
    pallas_call x1, Pallas kernels: 86 us -> 82.5 us  [local(): pl.pallas_call(functools.partial(kernel, XL, Y, ZC), out_shape=jax.ShapeD...]
where the time goes in v2:
time: 84.1 us; the launch traced here: 83.8 us
  Pallas kernels  82.5 us (98%)
  local copies, waits for them, and re-layouts  1.38 us (2%)
    pallas_call x1, Pallas kernels, local(): pl.pallas_call(functools.partial(kernel, XL, Y, ZC), out_shape=jax.ShapeD...  82.5 us

profile of v2, /device:TPU:1, one launch (start us, length us, event | category | flops | bytes accessed | tf_op | source)
XLA Modules:
  0.0 83.8 jit_solution(12189687659698420093)
XLA Ops:
  0.0 82.5 %shard_map.73 = bf16[128,128]{1,0:T(8,128)(2,1)} custom-call(bf16[128,128]{1,0:T(8,128)(2,1)} %tok_hbm.1, bf16[128,128]{1,0:T(8,128)(2,1)} %cot_hbm.1, s32[1,128]{1,0:T(1,128)} %bitcast.7, s32[1,128]{1,0:T(1,128)} %bitcast.8, f32[1,128]{1,0:T(1,128)} %bitcast.9, bf16[2,8,128,384]{3,2,1,0:T(8,128)(2,1)} %bitcast.5, bf16[384,2048]{1,0:T(8,128)(2,1)} %bitcast.6), custom_call_target="tpu_custom_call" | custom-call | flops 1207959552 | bytes 3145728 | tf_op jit(solution)/shard_map/pallas_call | solution.py:289
  82.5 1.4 %copy.9 = bf16[128,128]{1,0:T(8,128)(2,1)} copy(bf16[128,128]{1,0:T(8,128)(2,1)} %shard_map.73) | data formatting | bytes 65536

commit v3 on v2

--- a/solution.py
+++ b/solution.py
@@ -11,7 +11,7 @@
 F32 = jnp.float32
 BF16 = jnp.bfloat16
 CAP = 4
-WAVE = 4
+EARLY = {2: ((0, 1),), 4: ((1, 1), (2, 1)), 6: ((3, 1), (4, 1), (0, 2))}
 GROUP = 2
 VMEM_LIMIT = 63 * 1024 * 1024
 XH = 2
@@ -126,7 +126,8 @@
         return pl.ds(pl.multiple_of(lax.rem(zc + j, ZC) * span, span), span)
 
     others = pl.ds(0, total - span)
-    for j in range(1, ZC):
+    outward = sorted(range(1, ZC), key=lambda j: -min(j, ZC - j))
+    for j in outward:
         send(s1.at[:, zc_rows(j)], r1.at[:, zc_rows(0)], ssem.at[0], z1r.at[0], at_zc(j))
     r1[:, zc_rows(0)] = s1[:, zc_rows(0)]
     for load in loads:
@@ -177,20 +178,28 @@
             pre[...] += a
             inner[...] += b
 
-    waves = [near[i:i + WAVE] for i in range(0, X, WAVE)]
-    for j in near:
+    passed = set()
+
+    def pass_on(j, hop):
+        if (j, hop) in passed:
+            return
+        passed.add((j, hop))
+        for way in range(2):
+            ring(way, hop, j, 0)
+            if hop < H:
+                ring(way, hop + 1, j, 1)
+
+    for n, j in enumerate(near):
         if j:
             arrive(g.at[:, y, unit(-j)], ssem.at[1], x1r.at[j], at_x(j))
         for way in range(2):
             ring(way, 1, j, 1)
+        for k, hop in EARLY.get(n, ()):
+            pass_on(near[k], hop)
     for hop in range(1, H + 1):
-        for wave in waves:
-            for j in wave:
-                for way in range(2):
-                    ring(way, hop, j, 0)
-                    if hop < H:
-                        ring(way, hop + 1, j, 1)
-            if hop == 1 and wave is waves[0]:
+        for n, j in enumerate(near):
+            pass_on(j, hop)
+            if hop == 1 and n == X // 2:
                 for load in loads:
                     load.wait()
                 accumulate(y, True)
@@ -264,7 +273,7 @@
         ).astype(BF16)
     s4[...] = dot(perm, eg[...].reshape(total, feat), ((0,), (0,))).astype(BF16)
 
-    for j in range(1, ZC):
+    for j in outward:
         send(s4.at[zc_rows(j)], r4.at[zc_rows(0)], ssem.at[5], z2r.at[0], at_zc(j))
     r4[zc_rows(0)] = s4[zc_rows(0)]
     sent(s1.at[:, others], ssem.at[0], at_zc(1))

time: 84.1 us -> 82.4 us (0.980)
  Pallas kernels: 82.5 us -> 80.7 us
    pallas_call x1, Pallas kernels: 82.5 us -> 80.7 us  [local(): pl.pallas_call(functools.partial(kernel, XL, Y, ZC), out_shape=jax.ShapeD...]
where the time goes in v3:
time: 82.4 us; the launch traced here: 82.1 us
  Pallas kernels  80.7 us (98%)
  local copies, waits for them, and re-layouts  1.38 us (2%)
    pallas_call x1, Pallas kernels, local(): pl.pallas_call(functools.partial(kernel, XL, Y, ZC), out_shape=jax.ShapeD...  80.7 us

profile of v3, /device:TPU:1, one launch (start us, length us, event | category | flops | bytes accessed | tf_op | source)
XLA Modules:
  0.0 82.1 jit_solution(17559768371192684396)
XLA Ops:
  0.0 80.7 %shard_map.73 = bf16[128,128]{1,0:T(8,128)(2,1)} custom-call(bf16[128,128]{1,0:T(8,128)(2,1)} %tok_hbm.1, bf16[128,128]{1,0:T(8,128)(2,1)} %cot_hbm.1, s32[1,128]{1,0:T(1,128)} %bitcast.7, s32[1,128]{1,0:T(1,128)} %bitcast.8, f32[1,128]{1,0:T(1,128)} %bitcast.9, bf16[2,8,128,384]{3,2,1,0:T(8,128)(2,1)} %bitcast.5, bf16[384,2048]{1,0:T(8,128)(2,1)} %bitcast.6), custom_call_target="tpu_custom_call" | custom-call | flops 1207959552 | bytes 3145728 | tf_op jit(solution)/shard_map/pallas_call | solution.py:298
  80.8 1.4 %copy.9 = bf16[128,128]{1,0:T(8,128)(2,1)} copy(bf16[128,128]{1,0:T(8,128)(2,1)} %shard_map.73) | data formatting | bytes 65536

commit v4 on v3

--- a/solution.py
+++ b/solution.py
@@ -203,9 +203,11 @@
                 for load in loads:
                     load.wait()
                 accumulate(y, True)
-        accumulate(lax.rem(y + hop, Y))
-        if hop < H:
-            accumulate(lax.rem(y + Y - hop, Y))
+            elif hop > 1 and n == X // 4:
+                accumulate(lax.rem(y + hop - 1, Y))
+            elif hop > 1 and n == X - X // 4:
+                accumulate(lax.rem(y + Y - hop + 1, Y))
+    accumulate(lax.rem(y + H, Y))
 
     hg[...] = (inner[...] * gelu_slope(pre[...])).astype(BF16)
 

time: 82.4 us -> 82.5 us (level)
  no operation moved by 1% of the time
where the time goes in v4:
time: 82.5 us; the launch traced here: 82.2 us
  Pallas kernels  80.8 us (98%)
  local copies, waits for them, and re-layouts  1.38 us (2%)
    pallas_call x1, Pallas kernels, local(): pl.pallas_call(functools.partial(kernel, XL, Y, ZC), out_shape=jax.ShapeD...  80.8 us

profile of v4, /device:TPU:1, one launch (start us, length us, event | category | flops | bytes accessed | tf_op | source)
XLA Modules:
  0.0 82.2 jit_solution(11968888845320584286)
XLA Ops:
  0.0 80.8 %shard_map.73 = bf16[128,128]{1,0:T(8,128)(2,1)} custom-call(bf16[128,128]{1,0:T(8,128)(2,1)} %tok_hbm.1, bf16[128,128]{1,0:T(8,128)(2,1)} %cot_hbm.1, s32[1,128]{1,0:T(1,128)} %bitcast.7, s32[1,128]{1,0:T(1,128)} %bitcast.8, f32[1,128]{1,0:T(1,128)} %bitcast.9, bf16[2,8,128,384]{3,2,1,0:T(8,128)(2,1)} %bitcast.5, bf16[384,2048]{1,0:T(8,128)(2,1)} %bitcast.6), custom_call_target="tpu_custom_call" | custom-call | flops 1207959552 | bytes 3145728 | tf_op jit(solution)/shard_map/pallas_call | solution.py:300
  80.8 1.4 %copy.9 = bf16[128,128]{1,0:T(8,128)(2,1)} copy(bf16[128,128]{1,0:T(8,128)(2,1)} %shard_map.73) | data formatting | bytes 65536
